TPU v7x, 32 devices: a whole 2x2x4 slice. The times are simulated.
32 devices in a mesh: space: 16 (over z, y, x), sample: 2 (over core).
Axes of the slice: x: 2, y: 2, z: 4, core: 2. Of those that a mesh axis runs over, the one named last changes fastest.
Arguments:
- features: bfloat16 [2, 16, 1, 8, 8, 768], P('sample', 'space'), may hold values from -12 to 12
- wall_mask: int32 [2, 16, 1, 8, 64], P('sample', 'space'), may hold values 0 or 1
- block_positions: int32 [2, 16, 1], P('sample'), may hold values from -1 to 3, as said below
- dw_kernel: float32 [5, 5, 5, 96], replicated, may hold values from -0.5 to 0.5
- norm_gain: float32 [96], replicated, may hold values from 0.1 to 1.9
- norm_bias: float32 [96], replicated, may hold values from -3 to 3
- w_in: bfloat16 [96, 384], replicated, may hold values from -0.625 to 0.625
- b_in: float32 [384], replicated, may hold values from -3 to 3
- w_out: bfloat16 [384, 96], replicated, may hold values from -0.3125 to 0.3125
- b_out: float32 [96], replicated, may hold values from -3 to 3
- layer_scale: float32 [96], replicated, may hold values from 0.3 to 1.5
- upstream: bfloat16 [2, 16, 1, 8, 8, 768], P('sample', 'space'), may hold values from -6 to 6
Outputs:
- mixed: bfloat16 [2, 16, 1, 8, 8, 768], P('sample', 'space')
- grad_features: bfloat16 [2, 16, 1, 8, 8, 768], P('sample', 'space')
- grad_kernel: float32 [5, 5, 5, 96], replicated
- grad_w_in: float32 [96, 384], replicated
- grad_w_out: float32 [384, 96], replicated
- grad_b_in: float32 [384], replicated
- grad_vectors: float32 [4, 96], replicated
Inputs may be any that keep to these rules, and one draw needn't show every extreme that they name: `block_positions`: in each layer the live slots come first and hold distinct positions; each layer holds exactly 1 block, in slot 0; the first layer of every sample is full and holds position 3.
All inputs are finite; a program needn't handle non-finite values. No bound on the sum of `wall_mask` on one device may be relied on, other than what follows from the above.
Results may differ from a plain program's by a relative error of at most 0.007.
Values may be sent and summed in bfloat16 or wider, within the bound.
No kernel may reach another device: no remote copies, remote signals or barrier semaphores. Data moves between devices by JAX's collectives and lax.ppermute only.
A program may use at most 64 MiB of HBM per device.

v0:
```python
import math

import jax
import jax.numpy as jnp
from jax import lax
from jax.sharding import PartitionSpec as P

GRID = 2


GELU_SCALE = 0.7978845608028654
GELU_CUBIC = 0.044715
NORM_EPS = 1e-06


def with_halo(block, sides, width):
    for axis, dim in sides:
        count = lax.axis_size(axis)
        forward = [(i, i + 1) for i in range(count - 1)]
        backward = [(target, source) for source, target in forward]
        low = lax.ppermute(
            lax.slice_in_dim(block, block.shape[dim] - width, None, axis=dim), axis, forward
        )
        high = lax.ppermute(lax.slice_in_dim(block, 0, width, axis=dim), axis, backward)
        block = jnp.concatenate([low, block, high], axis=dim)
    return block


def gelu_value(pre_act):
    inner = GELU_SCALE * (pre_act + GELU_CUBIC * pre_act * pre_act * pre_act)
    return 0.5 * pre_act * (1.0 + jnp.tanh(inner))


def gelu_slope(pre_act):
    inner = GELU_SCALE * (pre_act + GELU_CUBIC * pre_act * pre_act * pre_act)
    tanh_value = jnp.tanh(inner)
    return 0.5 * (1.0 + tanh_value) + 0.5 * pre_act * (
        1.0 - tanh_value * tanh_value
    ) * GELU_SCALE * (1.0 + 3.0 * GELU_CUBIC * pre_act * pre_act)


def expand_fluid(wall_rows, channels):
    block_edge = wall_rows.shape[-2]
    lead_shape = wall_rows.shape[:-2]
    fluid_mask = (
        (1 - wall_rows)
        .astype(jnp.bfloat16)
        .reshape(lead_shape + (block_edge, block_edge, block_edge, 1))
    )
    fluid_mask = jnp.broadcast_to(
        fluid_mask, lead_shape + (block_edge, block_edge, block_edge, channels)
    )
    return fluid_mask.reshape(lead_shape + (block_edge, block_edge, block_edge * channels))


def edge_range(step_now, block_edge):
    if step_now < 0:
        return (block_edge - 2, block_edge)
    if step_now > 0:
        return (0, 2)
    return (0, block_edge)


def select_blocks(source, own_pos, source_pos, step_y, step_x, grid_side):
    own_y = own_pos // grid_side
    own_x = own_pos % grid_side
    target_y = own_y + step_y
    target_x = own_x + step_x
    inside = (
        (own_pos >= 0)
        & (target_y >= 0)
        & (target_y < grid_side)
        & (target_x >= 0)
        & (target_x < grid_side)
    )
    target = target_y * grid_side + target_x
    match = (source_pos[None, :] == target[:, None]) & inside[:, None] & (source_pos[None, :] >= 0)
    chosen = jnp.where(match[:, :, None, None, None], source[None], jnp.zeros((), source.dtype))
    return jnp.sum(chosen, axis=1)


def assemble(own_field, below_rims, above_rims, own_pos, below_pos, above_pos, grid_side):
    block_edge = own_field.shape[1]
    channels = own_field.shape[3] // block_edge
    row_parts = []
    for step_y in (-1, 0, 1):
        col_parts = []
        for step_x in (-1, 0, 1):
            y_low, y_high = edge_range(step_y, block_edge)
            x_low, x_high = edge_range(step_x, block_edge)
            pieces = []
            for source, source_pos in (
                (below_rims, below_pos),
                (own_field, own_pos),
                (above_rims, above_pos),
            ):
                trimmed = source[:, :, y_low:y_high, x_low * channels : x_high * channels]
                pieces.append(
                    select_blocks(trimmed, own_pos, source_pos, step_y, step_x, grid_side)
                )
            col_parts.append(jnp.concatenate(pieces, axis=1))
        row_parts.append(jnp.concatenate(col_parts, axis=3))
    return jnp.concatenate(row_parts, axis=2)


def depthwise(padded, dw_kernel, block_edge):
    channels = dw_kernel.shape[3]
    tap_count = dw_kernel.shape[0]
    running = jnp.zeros(
        (padded.shape[0], block_edge, block_edge, block_edge * channels), jnp.float32
    )
    for tap_z in range(tap_count):
        for tap_y in range(tap_count):
            for tap_x in range(tap_count):
                weight_row = jnp.tile(dw_kernel[tap_z, tap_y, tap_x], block_edge)
                window = padded[
                    :,
                    tap_z : tap_z + block_edge,
                    tap_y : tap_y + block_edge,
                    tap_x * channels : (tap_x + block_edge) * channels,
                ]
                running = running + window.astype(jnp.float32) * weight_row
    return running


def kernel_grad(padded, grad_conv, block_edge, tap_count):
    channels = padded.shape[3] // (block_edge + tap_count - 1)
    grad_wide = grad_conv.astype(jnp.float32)
    rows_list = []
    for tap_z in range(tap_count):
        for tap_y in range(tap_count):
            for tap_x in range(tap_count):
                window = padded[
                    :,
                    tap_z : tap_z + block_edge,
                    tap_y : tap_y + block_edge,
                    tap_x * channels : (tap_x + block_edge) * channels,
                ]
                per_lane = jnp.sum(window.astype(jnp.float32) * grad_wide, axis=(0, 1, 2))
                rows_list.append(jnp.sum(per_lane.reshape(block_edge, channels), axis=0))
    return jnp.stack(rows_list).reshape(tap_count, tap_count, tap_count, channels)


def dense_step(
    conv_slot,
    field_slot,
    live_value,
    upstream_slot,
    norm_gain,
    norm_bias,
    w_in,
    b_in,
    w_out,
    b_out,
    layer_scale,
):
    channels = norm_gain.shape[0]
    slot_shape = field_slot.shape
    conv_rows = conv_slot.reshape(-1, channels)
    row_mean = jnp.mean(conv_rows, axis=1, keepdims=True)
    centred = conv_rows - row_mean
    row_var = jnp.mean(centred * centred, axis=1, keepdims=True)
    inv_std = lax.rsqrt(row_var + NORM_EPS)
    unit_rows = centred * inv_std
    normed = (unit_rows * norm_gain + norm_bias).astype(jnp.bfloat16)
    pre_act = jnp.dot(normed, w_in, preferred_element_type=jnp.float32) + b_in
    activated = gelu_value(pre_act).astype(jnp.bfloat16)
    branch = jnp.dot(activated, w_out, preferred_element_type=jnp.float32) + b_out
    field_rows = field_slot.reshape(-1, channels).astype(jnp.float32)
    mixed = ((field_rows + layer_scale * branch) * live_value).astype(jnp.bfloat16)
    seed_grad = upstream_slot.reshape(-1, channels).astype(jnp.float32) * live_value
    scale_grad = jnp.sum(seed_grad * branch, axis=0)
    grad_branch = (seed_grad * layer_scale).astype(jnp.bfloat16)
    bout_grad = jnp.sum(grad_branch.astype(jnp.float32), axis=0)
    wout_grad = jnp.dot(activated.T, grad_branch, preferred_element_type=jnp.float32)
    grad_act = jnp.dot(grad_branch, w_out.T, preferred_element_type=jnp.float32)
    grad_pre = (grad_act * gelu_slope(pre_act)).astype(jnp.bfloat16)
    bin_grad = jnp.sum(grad_pre.astype(jnp.float32), axis=0)
    win_grad = jnp.dot(normed.T, grad_pre, preferred_element_type=jnp.float32)
    grad_normed = jnp.dot(grad_pre, w_in.T, preferred_element_type=jnp.float32)
    gain_grad = jnp.sum(grad_normed * unit_rows, axis=0)
    bias_grad = jnp.sum(grad_normed, axis=0)
    scaled = grad_normed * norm_gain
    grad_conv = inv_std * (
        scaled
        - jnp.mean(scaled, axis=1, keepdims=True)
        - unit_rows * jnp.mean(scaled * unit_rows, axis=1, keepdims=True)
    )
    grad_conv = grad_conv.astype(jnp.bfloat16).reshape(slot_shape)
    vectors = jnp.stack([gain_grad, bias_grad, bout_grad, scale_grad])
    return (mixed.reshape(slot_shape), grad_conv, (win_grad, wout_grad, bin_grad, vectors))


def local(
    features,
    wall_mask,
    block_positions,
    dw_kernel,
    norm_gain,
    norm_bias,
    w_in,
    b_in,
    w_out,
    b_out,
    layer_scale,
    upstream,
):
    own_field = features[0, 0]
    own_walls = wall_mask[0, 0]
    own_upstream = upstream[0, 0]
    position_table = block_positions[0]
    slot_count = own_field.shape[0]
    block_edge = own_field.shape[1]
    channels = dw_kernel.shape[3]
    tap_count = dw_kernel.shape[0]
    layer_index = lax.axis_index("space")
    layer_count = lax.axis_size("space")
    own_pos = lax.dynamic_index_in_dim(position_table, layer_index, 0, keepdims=False)
    low_row = lax.dynamic_index_in_dim(
        position_table, jnp.maximum(layer_index - 1, 0), 0, keepdims=False
    )
    high_row = lax.dynamic_index_in_dim(
        position_table, jnp.minimum(layer_index + 1, layer_count - 1), 0, keepdims=False
    )
    below_pos = jnp.where(layer_index > 0, low_row, -1)
    above_pos = jnp.where(layer_index < layer_count - 1, high_row, -1)
    live_flag = (own_pos >= 0).astype(jnp.bfloat16)
    fluid_mask = expand_fluid(own_walls, channels)
    masked = own_field * fluid_mask * live_flag[:, None, None, None]
    rims = jnp.concatenate([masked[:, :2], masked[:, block_edge - 2 :]], axis=1)
    extended = with_halo(rims, (("space", 1),), 2)
    padded = assemble(masked, extended[:, :2], extended[:, 6:], own_pos, below_pos, above_pos, GRID)
    conv_out = depthwise(padded, dw_kernel, block_edge)

    def slot_step(slot_items):
        return dense_step(
            slot_items[0],
            slot_items[1],
            slot_items[2],
            slot_items[3],
            norm_gain,
            norm_bias,
            w_in,
            b_in,
            w_out,
            b_out,
            layer_scale,
        )

    mixed, grad_conv, grads = lax.map(
        slot_step, (conv_out, own_field, live_flag.astype(jnp.float32), own_upstream)
    )
    grad_rims = jnp.concatenate([grad_conv[:, :2], grad_conv[:, block_edge - 2 :]], axis=1)
    grad_extended = with_halo(grad_rims, (("space", 1),), 2)
    grad_padded = assemble(
        grad_conv, grad_extended[:, :2], grad_extended[:, 6:], own_pos, below_pos, above_pos, GRID
    )
    back_conv = depthwise(grad_padded, dw_kernel[::-1, ::-1, ::-1], block_edge)
    live_wide = live_flag.astype(jnp.float32)[:, None, None, None]
    seed_grad = own_upstream.astype(jnp.float32) * live_wide
    grad_field = (seed_grad + back_conv * fluid_mask * live_wide).astype(jnp.bfloat16)
    kernel_term = kernel_grad(padded, grad_conv, block_edge, tap_count)
    local_parts = (
        kernel_term,
        jnp.sum(grads[0], axis=0),
        jnp.sum(grads[1], axis=0),
        jnp.sum(grads[2], axis=0),
        jnp.sum(grads[3], axis=0),
    )
    totals = lax.psum(
        (local_parts[0], local_parts[1], local_parts[2], local_parts[3], local_parts[4]),
        ("space", "sample"),
    )
    voxel_total = layer_count * lax.axis_size("sample") * slot_count * block_edge**3
    factor = 1.0 / math.sqrt(voxel_total)
    return (
        mixed[None, None],
        grad_field[None, None],
        totals[0] * factor,
        totals[1] * factor,
        totals[2] * factor,
        totals[3] * factor,
        totals[4] * factor,
    )


def solution(mesh):
    return jax.shard_map(
        local,
        mesh=mesh,
        in_specs=(
            P("sample", "space", None, None, None, None),
            P("sample", "space", None, None, None),
            P("sample", None, None),
            P(),
            P(),
            P(),
            P(),
            P(),
            P(),
            P(),
            P(),
            P("sample", "space", None, None, None, None),
        ),
        out_specs=(
            P("sample", "space", None, None, None, None),
            P("sample", "space", None, None, None, None),
            P(),
            P(),
            P(),
            P(),
            P(),
        ),
        check_vma=False,
    )
```

profile of v0, /device:TPU:1, one launch (start us, length us, event | category | flops | bytes accessed | tf_op | source)
XLA Modules:
  0.0 270.8 jit_solution(2417540304864938514)
XLA Ops:
  13.5 0.7 copy-done.2
  14.3 4.1 %collective-permute-start = (bf16[1,2,8,768]{3,2,1,0:T(8,128)(2,1)S(1)}, bf16[1,2,8,768]{3,2,1,0:T(8,128)(2,1)S(1)}, u32[]{:S(2)}, u32[]{:S(2)}) collective-permute-start(bf16[1,2,8,768]{3,2,1,0:T(8,128)(2,1)S(1)} %get-tuple-element.352), channel_id=1, source_target_pairs={{0,2},{2,4},{4,6},{6,8},{8,10},{10,12},{12,14},{14,16},{16,18},{18... | collective-permute-start | bytes 73736 | tf_op jit(solution)/shard_map/ppermute | solution.py:21
  18.4 1.3 collective-permute-start.1
  25.3 0.7 copy-done.1
  39.6 13.9 %fusion.129 = f32[1,8,8,768]{3,2,1,0:T(8,128)S(1)} fusion(bf16[1,8,8,768]{3,2,1,0:T(8,128)(2,1)S(1)} %get-tuple-element.199, bf16[1,2,8,768]{3,2,1,0:T(8,128)(2,1)S(1)} %broadcast_select_fusion.7, bf16[1,2,8,768]{3,2,1,0:T(8,128)(2,1)S(1)} %broadcast_select_fusion.9, f32[768]{0:T(1024)S(1)} %mul.3130, f32[768]{0:T(1024)S(1)} %mul.3127, f32[768]{0:T(1024)S(1)} %mul.3124, ...), kind=kLoop, calls=%fused_computation.778 | loop fusion | flops 33718272 | bytes 3025920 | tf_op jit(solution)/shard_map/add | solution.py:122
  56.3 0.9 fusion.462
  57.8 0.9 fusion.458
  62.0 0.9 fusion.236
  62.9 0.9 fusion.250
  63.7 0.8 fusion.251
  64.5 1.0 fusion.252
  65.6 0.9 fusion.253
  66.5 0.8 fusion.254
  67.3 0.8 fusion.238
  68.2 0.9 fusion.239
  69.1 1.1 fusion.237
  82.7 43.1 %all-reduce = (f32[5,5,5,96]{3,2,1,0:T(8,128)S(1)}, f32[384]{0:T(512)S(1)}, f32[4,96]{1,0:T(4,128)S(1)}) all-reduce(f32[5,5,5,96]{3,2,1,0:T(8,128)S(1)} %reshape.2288, f32[384]{0:T(512)S(1)} %get-tuple-element.392, f32[4,96]{1,0:T(4,128)S(1)} %pad_maximum_fusion.26), channel_id=1, replica_groups=mesh['space'=16,'sample'=2] {'space','sample'}, use_global_device_ids=true, to_apply=%region_254.255 | all-reduce | flops 12768 | bytes 102144 | tf_op jit(solution)/shard_map/psum | solution.py:270
  127.1 3.0 %collective-permute-start.2 = (bf16[1,2,8,768]{3,2,1,0:T(8,128)(2,1)S(1)}, bf16[1,2,8,768]{3,2,1,0:T(8,128)(2,1)S(1)}, u32[]{:S(2)}, u32[]{:S(2)}) collective-permute-start(bf16[1,2,8,768]{3,2,1,0:T(8,128)(2,1)S(1)} %get-tuple-element.342), channel_id=1, source_target_pairs={{0,2},{2,4},{4,6},{6,8},{8,10},{10,12},{12,14},{14,16},{16,18},{18... | collective-permute-start | bytes 73736 | tf_op jit(solution)/shard_map/ppermute | solution.py:21
  130.8 0.8 broadcast_in_dim.881
  131.6 1.3 collective-permute-start.3
  133.0 3.2 %collective-permute-done.3 = bf16[1,2,8,768]{3,2,1,0:T(8,128)(2,1)S(1)} collective-permute-done((bf16[1,2,8,768]{3,2,1,0:T(8,128)(2,1)S(1)}, bf16[1,2,8,768]{3,2,1,0:T(8,128)(2,1)S(1)}, u32[]{:S(2)}, u32[]{:S(2)}) %collective-permute-start.3) | collective-permute-done | bytes 24608 | tf_op jit(solution)/shard_map/ppermute | solution.py:24
  137.7 15.2 %fusion.457 = bf16[1,1,1,8,8,768]{5,4,3,2,1,0:T(8,128)(2,1)} fusion(f32[]{:T(128)S(6)} %squeeze.34, bf16[1,8,8,768]{3,2,1,0:T(8,128)(2,1)S(1)} %broadcast_in_dim.803, f32[768]{0:T(1024)S(1)} %mul.2757, f32[768]{0:T(1024)S(1)} %mul.2760, f32[768]{0:T(1024)S(1)} %mul.2763, f32[768]{0:T(1024)S(1)} %mul.2766, f32[768]{0:T(1024)S(1)} %mul.2769, ...), kind=kLoop, calls=%fused_computation.1144 | loop fusion | flops 34062336 | bytes 3125248 | tf_op jit(solution)/shard_map/broadcast_in_dim | solution.py:278
  152.8 108.8 %all-reduce.4.cloned.1.call-done = (f32[96,384]{1,0:T(8,128)}, f32[384,96]{0,1:T(8,128)}) async-done(((f32[96,384]{1,0:T(8,128)}, f32[384,96]{0,1:T(8,128)}), (f32[96,384]{1,0:T(8,128)}, f32[384,96]{0,1:T(8,128)})) %all-reduce.4.cloned.1.call-update) | async-done | bytes 294928 | tf_op jit(solution)/shard_map/psum | solution.py:270
  261.6 1.6 broadcast_multiply_fusion.1
  (623 shorter events, 36.6 us)
Async XLA Ops:
  7.2 46.8 %copy-start = (bf16[96,384]{1,0:T(8,128)(2,1)S(1)}, bf16[96,384]{1,0:T(8,128)(2,1)}, u32[]{:S(2)}) copy-start(bf16[96,384]{1,0:T(8,128)(2,1)} %param.18) | copy-start | bytes 221188
  7.2 254.5 %all-reduce.4.cloned.1.call-start = ((), (), s32[]{:S(2)}) async-start(), calls=%async_computation | async-start | bytes 589824 | tf_op jit(solution)/shard_map/psum | solution.py:270
  7.2 0.7 copy-start.6
  11.8 1.3 copy-start.8
  13.3 0.9 copy-start.2
  14.2 5.5 %copy-start.5 = (f32[5,5,5,96]{3,2,1,0:T(8,128)S(1)}, f32[5,5,5,96]{3,2,1,0:T(8,128)}, u32[]{:S(2)}) copy-start(f32[5,5,5,96]{3,2,1,0:T(8,128)} %param.15) | copy-start | bytes 144004
  14.3 23.7 %collective-permute-start = (bf16[1,2,8,768]{3,2,1,0:T(8,128)(2,1)S(1)}, bf16[1,2,8,768]{3,2,1,0:T(8,128)(2,1)S(1)}, u32[]{:S(2)}, u32[]{:S(2)}) collective-permute-start(bf16[1,2,8,768]{3,2,1,0:T(8,128)(2,1)S(1)} %get-tuple-element.352), channel_id=1, source_target_pairs={{0,2},{2,4},{4,6},{6,8},{8,10},{10,12},{12,14},{14,16},{16,18},{18... | collective-permute-start | bytes 73736 | tf_op jit(solution)/shard_map/ppermute | solution.py:21
  18.4 19.7 %collective-permute-start.1 = (bf16[1,2,8,768]{3,2,1,0:T(8,128)(2,1)S(1)}, bf16[1,2,8,768]{3,2,1,0:T(8,128)(2,1)S(1)}, u32[]{:S(2)}, u32[]{:S(2)}) collective-permute-start(bf16[1,2,8,768]{3,2,1,0:T(8,128)(2,1)S(1)} %get-tuple-element.353), channel_id=1, source_target_pairs={{2,0},{4,2},{6,4},{8,6},{10,8},{12,10},{14,12},{16,14},{18,16},{20... | collective-permute-start | bytes 73736 | tf_op jit(solution)/shard_map/ppermute | solution.py:24
  25.1 0.9 copy-start.1
  54.0 0.7 copy-start.7
  54.0 0.7 copy-start.11
  54.0 0.7 copy-start.12
  54.7 0.9 copy-start.4
  55.2 0.7 copy-start.9
  55.3 0.7 copy-start.10
  127.1 5.8 %collective-permute-start.2 = (bf16[1,2,8,768]{3,2,1,0:T(8,128)(2,1)S(1)}, bf16[1,2,8,768]{3,2,1,0:T(8,128)(2,1)S(1)}, u32[]{:S(2)}, u32[]{:S(2)}) collective-permute-start(bf16[1,2,8,768]{3,2,1,0:T(8,128)(2,1)S(1)} %get-tuple-element.342), channel_id=1, source_target_pairs={{0,2},{2,4},{4,6},{6,8},{8,10},{10,12},{12,14},{14,16},{16,18},{18... | collective-permute-start | bytes 73736 | tf_op jit(solution)/shard_map/ppermute | solution.py:21
  131.6 4.6 %collective-permute-start.3 = (bf16[1,2,8,768]{3,2,1,0:T(8,128)(2,1)S(1)}, bf16[1,2,8,768]{3,2,1,0:T(8,128)(2,1)S(1)}, u32[]{:S(2)}, u32[]{:S(2)}) collective-permute-start(bf16[1,2,8,768]{3,2,1,0:T(8,128)(2,1)S(1)} %get-tuple-element.343), channel_id=1, source_target_pairs={{2,0},{4,2},{6,4},{8,6},{10,8},{12,10},{14,12},{16,14},{18,16},{20... | collective-permute-start | bytes 73736 | tf_op jit(solution)/shard_map/ppermute | solution.py:24
  261.6 1.6 copy-start.3
Sparse Core Ops, SparseCore 0:
  133.0 128.5 all-reduce.3
where the time goes:
time: 273 us; the launch traced here: 271 us
  waiting for transfers between devices  112 us (41%)
  other arithmetic  48.8 us (18%)
  blocking collectives  43.1 us (16%)
  local copies, waits for them, and re-layouts  26.8 us (10%)
  between operations  26.5 us (10%)
  starting transfers between devices  9.69 us (4%)
  matrix products  3.79 us (1%)
    psum x1, waiting for transfers between devices, local(): lax.psum((local_parts[0], local_parts[1], local_parts[2], local_parts[3],...  109 us
    psum x1, blocking collectives, local(): lax.psum((local_parts[0], local_parts[1], local_parts[2], local_parts[3],...  43.1 us
    broadcast_in_dim x1, other arithmetic, local(): grad_field[None, None]  15.2 us
    add x1, other arithmetic, depthwise(): running = running + window.astype(jnp.float32) * weight_row  13.9 us
    reduce_sum x15, other arithmetic, kernel_grad(): per_lane = jnp.sum(window.astype(jnp.float32) * grad_wide, axis=(0, 1, 2))  10.4 us
    mul x125, local copies, waits for them, and re-layouts, depthwise(): running = running + window.astype(jnp.float32) * weight_row  9.46 us
    reshape x125, local copies, waits for them, and re-layouts, kernel_grad(): rows_list.append(jnp.sum(per_lane.reshape(block_edge, channels), axis=0))  8.94 us
    ppermute x2, starting transfers between devices, with_halo(): lax.ppermute(lax.slice_in_dim(block, block.shape[dim] - width, None, axis...  7.08 us
  transfers between devices with their start and end apart: 5, of which 2 were waited for; matrix products, arithmetic and copies ran while one was open for 11% of the time, Pallas kernels for 0%

commit v1 on v0

v1 whole, which is shorter than its diff:
```python
import functools
import math

import jax
import jax.numpy as jnp
from jax import lax
from jax.experimental import pallas as pl
from jax.experimental.pallas import tpu as pltpu
from jax.sharding import PartitionSpec as P

GELU_SCALE = 0.7978845608028654
GELU_CUBIC = 0.044715
NORM_EPS = 1e-06

B = 8
T = 5
C = 96
HID = 384
LANES = 128

ROW_IN = 0
ROW_OUT = 288
ROW_KERNEL = 576
ROW_BIN = 704
ROW_VEC = 707
ROWS = 712

F32 = jnp.float32
BF16 = jnp.bfloat16

VMEM_LIMIT = 48 * 1024 * 1024


def params():
    return pltpu.CompilerParams(vmem_limit_bytes=VMEM_LIMIT)


def vmem():
    return pl.BlockSpec(memory_space=pltpu.VMEM)


def hbm():
    return pl.BlockSpec(memory_space=pltpu.HBM)


def pinned(array):
    return pltpu.with_memory_space_constraint(array, pltpu.HBM)


def start_copies(sems, *pairs):
    copies = [
        pltpu.make_async_copy(source, target, sems.at[k])
        for k, (source, target) in enumerate(pairs)
    ]
    for copy in copies:
        copy.start()
    return copies


def layer_places(table_ref):
    layer = lax.axis_index("space")
    count = lax.axis_size("space")
    own = table_ref[layer]
    low = table_ref[jnp.maximum(layer - 1, 0)]
    high = table_ref[jnp.minimum(layer + 1, count - 1)]
    live = jnp.where(own >= 0, 1.0, 0.0).astype(F32)
    return jnp.maximum(own, 0), jnp.maximum(low, 0), jnp.maximum(high, 0), live


def is_even():
    return (lax.axis_index("space") & 1) == 0


def halo_planes(even_ref, odd_ref):
    even = is_even()

    def low(k):
        return jnp.where(even, odd_ref[k].astype(F32), even_ref[k].astype(F32))

    def high(k):
        return jnp.where(even, even_ref[k].astype(F32), odd_ref[k].astype(F32))

    return low, high


def offset(own, other):
    dy = (other >> 1) - (own >> 1)
    dx = (other & 1) - (own & 1)
    return 8 * dx, 8 * dy


def spread(field):
    return [field[:, x * C : (x + 1) * C] for x in range(B)]


def gather_lanes(parts):
    return jnp.concatenate(parts, axis=-1)


def send_kernel(
    table_hbm,
    feat_hbm,
    wall_hbm,
    up_hbm,
    dw_hbm,
    even_ref,
    odd_ref,
    masked_ref,
    fluid_ref,
    dw_ref,
    table_ref,
    feat_ref,
    wall_ref,
    up_ref,
    sems,
):
    copies = start_copies(
        sems,
        (wall_hbm, wall_ref),
        (feat_hbm, feat_ref),
        (up_hbm, up_ref),
        (table_hbm, table_ref),
        (dw_hbm, dw_ref),
    )
    copies[3].wait()
    _, _, _, live = layer_places(table_ref)
    copies[0].wait()
    walls = wall_ref[...]
    fluid = (1 - walls).astype(F32)
    row = lax.broadcasted_iota(jnp.int32, (B, B * B), 0)
    lane = lax.broadcasted_iota(jnp.int32, (B, B * B), 1)
    pick = (lane >> 3) == row
    tall = jnp.concatenate(
        [jnp.where(pick, fluid[z : z + 1, :], 0.0) for z in range(B)], axis=0
    ).astype(BF16)
    src = lax.broadcasted_iota(jnp.int32, (B * B, B * C), 0) & 7
    dst = lax.broadcasted_iota(jnp.int32, (B * B, B * C), 1)
    widen = jnp.where((dst >= src * C) & (dst < src * C + C), 1.0, 0.0).astype(BF16)
    wide = jnp.dot(tall, widen, preferred_element_type=F32)
    copies[1].wait()
    copies[2].wait()
    for z in range(B):
        fluid_z = wide[z * B : (z + 1) * B, :]
        fluid_ref[z] = fluid_z.astype(BF16)
        masked = (feat_ref[z].astype(F32) * (fluid_z * live)).astype(BF16)
        masked_ref[z] = masked

    def payload(target, first):
        target[0:4] = masked_ref[first : first + 4]
        for k in range(2):
            plane = k if first == 0 else 6 + k
            target[4 + k] = (up_ref[plane].astype(F32) * live).astype(BF16)

    @pl.when(is_even())
    def _():
        payload(even_ref, 4)
        payload(odd_ref, 0)

    @pl.when(jnp.logical_not(is_even()))
    def _():
        payload(even_ref, 0)
        payload(odd_ref, 4)

    copies[4].wait()


def wide_taps(dw_ref, taps):
    for a in range(T):
        for b in range(T):
            for e in range(T):
                taps[a, b, e] = jnp.broadcast_to(dw_ref[a, b, e : e + 1, :], (B, C))


class Flipped:
    def __init__(self, taps):
        self.taps = taps

    def __getitem__(self, index):
        a, b, e = index
        return self.taps[T - 1 - a, T - 1 - b, T - 1 - e]


def rows_of():
    return lax.broadcasted_iota(jnp.int32, (B, C), 0)


def put_halo(halo, plane, parts, start):
    for x in range(B):
        halo[plane, start + 10 + x] = parts[x]


def clear_halo(halo, planes):
    for p in range(planes):
        halo[p, 8:20] = jnp.zeros((12, B, C), F32)


def add_own(acc, window, taps, a, b):
    for e in range(T):
        weight = taps[a, b, e]
        for x in range(B):
            if 0 <= x + e - 2 < B:
                acc[x] = acc[x] + window[x + e - 2] * weight


def add_halo(acc, window, taps, a, b):
    for e in range(T):
        weight = taps[a, b, e]
        for x in range(B):
            acc[x] = acc[x] + window[x + e] * weight


def row_masks(start=None):
    masks = []
    for by in range(-2, 3):
        row = rows_of() + by if start is None else rows_of() + (by - start)
        inside = (row >= 0) & (row < B)
        masks.append(None if start is None and by == 0 else jnp.where(inside, 1.0, 0.0))
    return masks


def shift_rows(value, by, masks):
    rolled = value if by == 0 else pltpu.roll(value, (-by) % B, 0)
    mask = masks[by + 2]
    return rolled if mask is None else rolled * mask


def conv_plane(source, taps, own, masks, halo=None, halos=(), halo_masks=None):
    out = [jnp.zeros((B, C), F32) for _ in range(B)]
    for b in range(T):
        if own:
            acc = [jnp.zeros((B, C), F32) for _ in range(B)]
            for a, plane in own:
                add_own(acc, [source[plane, x] for x in range(B)], taps, a, b)
            for x in range(B):
                out[x] = out[x] + shift_rows(acc[x], b - 2, masks)
        if halos:
            acc = [jnp.zeros((B, C), F32) for _ in range(B)]
            for a, plane in halos:
                add_halo(acc, [halo[plane, 8 + j] for j in range(12)], taps, a, b)
            for x in range(B):
                out[x] = out[x] + shift_rows(acc[x], b - 2, halo_masks)
    return out


def middle_plane(source, taps, first, masks):
    return conv_plane(source, taps, [(a, first + a) for a in range(T)], masks)


OWN_TAPS = {0: (2, 3, 4), 1: (1, 2, 3, 4), 6: (0, 1, 2, 3), 7: (0, 1, 2)}


def own_pairs(plane):
    return [(a, plane + a - 2) for a in OWN_TAPS.get(plane, range(T))]


def dense_weights(refs):
    gain, bias, w_in, b_in, w_out, b_out, scale = refs
    b_out = None if b_out is None else b_out[...]
    return (
        gain[...],
        bias[...],
        w_in[...],
        b_in[...].reshape(1, HID),
        w_out[...],
        b_out,
        scale[...],
    )


def dense_part(conv_rows, seed, weights, own=True):
    gain, bias, w_in, b_in, w_out_t, b_out, scale = weights
    mean = jnp.sum(conv_rows, axis=1, keepdims=True) * (1.0 / C)
    centred = conv_rows - mean
    var = jnp.sum(centred * centred, axis=1, keepdims=True) * (1.0 / C)
    inv_std = lax.rsqrt(var + NORM_EPS)
    unit = centred * inv_std
    normed = (unit * gain + bias).astype(BF16)
    pre = jnp.dot(normed, w_in, preferred_element_type=F32) + b_in
    square = pre * pre
    inner = pre * (GELU_SCALE + (GELU_SCALE * GELU_CUBIC) * square)
    tanh = jnp.tanh(inner)
    half = 0.5 + 0.5 * tanh
    slope = half + (0.5 * pre) * (1.0 - tanh * tanh) * (
        GELU_SCALE + (3.0 * GELU_SCALE * GELU_CUBIC) * square
    )
    grad_branch = (seed * scale).astype(BF16)
    grad_act = jnp.dot(grad_branch, w_out_t, preferred_element_type=F32)
    grad_pre = (grad_act * slope).astype(BF16)
    grad_normed = lax.dot_general(
        grad_pre, w_in, (((1,), (1,)), ((), ())), preferred_element_type=F32
    )
    scaled = grad_normed * gain
    mean_s = jnp.sum(scaled, axis=1, keepdims=True) * (1.0 / C)
    mean_su = jnp.sum(scaled * unit, axis=1, keepdims=True) * (1.0 / C)
    grad_conv = inv_std * (scaled - mean_s - unit * mean_su)
    grad_conv = grad_conv.astype(BF16).astype(F32).reshape(-1, B, B, C)
    if not own:
        return grad_conv
    activated = (pre * half).astype(BF16)
    branch = (
        lax.dot_general(activated, w_out_t, (((1,), (1,)), ((), ())), preferred_element_type=F32)
        + b_out
    )
    grad_in = lax.dot_general(
        normed, grad_pre, (((0,), (0,)), ((), ())), preferred_element_type=F32
    )
    grad_out = lax.dot_general(
        grad_branch, activated, (((0,), (0,)), ((), ())), preferred_element_type=F32
    )
    vec = jnp.concatenate(
        [
            jnp.sum(grad_normed * unit, axis=0, keepdims=True),
            jnp.sum(grad_normed, axis=0, keepdims=True),
            jnp.sum(grad_branch.astype(F32), axis=0, keepdims=True),
            jnp.sum(seed * branch, axis=0, keepdims=True),
        ],
        axis=0,
    )
    bin_sum = jnp.sum(grad_pre.astype(F32), axis=0, keepdims=True)
    return grad_conv, branch.reshape(-1, B, B, C), grad_in, grad_out, vec, bin_sum


def kernel_taps(pairs):
    acc = [[jnp.zeros((B, C), F32) for _ in range(2)] for _ in range(T)]
    for grads, window, inside in pairs:
        for e in range(T):
            for x in range(B):
                if inside:
                    if not 0 <= x + e - 2 < B:
                        continue
                    value = window[x + e - 2]
                else:
                    value = window[x + e]
                acc[e][x & 1] = acc[e][x & 1] + value * grads[x]
    return [pair[0] + pair[1] for pair in acc]


def move_rows(grads, moved, k, masks):
    for x in range(B):
        for b in range(T):
            moved[b, k, x] = shift_rows(grads[x], 2 - b, masks)


def early_kernel(
    masked_ref,
    dw_ref,
    table_hbm,
    up_hbm,
    gain_hbm,
    bias_hbm,
    w_in_hbm,
    b_in_hbm,
    w_out_hbm,
    b_out_hbm,
    scale_hbm,
    source,
    seeds,
    taps,
    conv,
    gain_ref,
    bias_ref,
    w_in_ref,
    b_in_ref,
    w_out_ref,
    b_out_ref,
    scale_ref,
    gc_ref,
    branch_ref,
    grad_in_ref,
    grad_out_ref,
    vec_ref,
    bin_ref,
    rows_ref,
    table_vmem,
    table_ref,
    up_ref,
    moved,
    sems,
):
    copies = start_copies(
        sems,
        (table_hbm, table_ref),
        (up_hbm, up_ref),
        (gain_hbm, gain_ref),
        (bias_hbm, bias_ref),
        (w_in_hbm, w_in_ref),
        (b_in_hbm, b_in_ref),
        (w_out_hbm, w_out_ref),
        (b_out_hbm, b_out_ref),
        (scale_hbm, scale_ref),
        (table_hbm, table_vmem),
    )

    def own_planes(z, carry):
        field = spread(masked_ref[z].astype(F32))
        for x in range(B):
            source[z, x] = field[x]
        return carry

    lax.fori_loop(0, B, own_planes, 0, unroll=True)
    wide_taps(dw_ref, taps)
    masks = row_masks()

    def middle_step(z, carry):
        out = middle_plane(source, taps, z, masks)
        for x in range(B):
            conv[2 + z, x] = out[x]
        return carry

    lax.fori_loop(0, 4, middle_step, 0)

    def edge(plane):
        out = conv_plane(source, taps, own_pairs(plane), masks)
        for x in range(B):
            conv[plane, x] = out[x]

    for plane in (0, 1, 6, 7):
        edge(plane)
    for copy in copies:
        copy.wait()
    live = layer_places(table_ref)[3]

    def own_seeds(z, carry):
        seed = spread(up_ref[z].astype(F32) * live)
        for x in range(B):
            seeds[z, x] = seed[x]
        return carry

    lax.fori_loop(0, B, own_seeds, 0, unroll=True)
    refs = (gain_ref, bias_ref, w_in_ref, b_in_ref, w_out_ref, b_out_ref, scale_ref)
    grad_conv, branch, grad_in, grad_out, vec, bin_sum = dense_part(
        conv[2:6].reshape(256, C), seeds[2:6].reshape(256, C), dense_weights(refs)
    )
    gc_ref[...] = grad_conv
    branch_ref[...] = branch
    grad_in_ref[...] = grad_in
    grad_out_ref[...] = grad_out
    vec_ref[...] = vec
    bin_ref[...] = bin_sum

    for k in range(4):
        move_rows([gc_ref[k, x] for x in range(B)], moved, k, masks)

    def kernel_step(b, carry):
        for a in range(T):
            sums = kernel_taps(
                (
                    [moved[b, k, x] for x in range(B)],
                    [source[k + a, x] for x in range(B)],
                    True,
                )
                for k in range(4)
            )
            for e in range(T):
                rows_ref[a * T + b, e] = sums[e]
        return carry

    lax.fori_loop(0, T, kernel_step, 0)


NEAR = {0: [(0, 0), (1, 1)], 1: [(0, 1)], 6: [(4, 2)], 7: [(3, 2), (4, 3)]}


def main_kernel(
    chunk,
    parts,
    odd_ref,
    even_ref,
    source,
    seeds,
    taps,
    conv_ref,
    gain_ref,
    bias_ref,
    w_in_ref,
    b_in_ref,
    w_out_ref,
    b_out_ref,
    scale_ref,
    early_gc,
    early_branch,
    early_in,
    early_out,
    early_vec,
    early_bin,
    early_rows,
    table_vmem,
    branch_ref,
    gc_ref,
    packed_ref,
    table_ref,
    sems,
    halo,
    conv,
    moved,
    moved_halo,
    kernel_rows,
    pack,
):
    copies = start_copies(sems, (table_vmem, table_ref))
    clear_halo(halo, 4)
    pack[ROW_KERNEL:ROWS, :] = jnp.zeros((ROWS - ROW_KERNEL, LANES), F32)
    gc_ref[2:6] = early_gc[...]
    branch_ref[2:6] = early_branch[...]

    from_low, from_high = halo_planes(even_ref, odd_ref)
    below = [spread(from_low(2 + k)) for k in range(2)]
    above = [spread(from_high(k)) for k in range(2)]
    copies[0].wait()
    own, low, high, _ = layer_places(table_ref)
    low_x, low_y = offset(own, low)
    high_x, high_y = offset(own, high)
    for k in range(2):
        put_halo(halo, k, below[k], low_x)
        put_halo(halo, 2 + k, above[k], high_x)
    low_masks, high_masks = row_masks(low_y), row_masks(high_y)
    for k, plane in enumerate((0, 1, 6, 7)):
        near = low_masks if k < 2 else high_masks
        out = conv_plane(source, taps, [], None, halo, NEAR[plane], near)
        for x in range(B):
            conv[k, x] = conv_ref[plane, x] + out[x]

    late = jnp.concatenate([seeds[0:2], seeds[6:8]], axis=0)
    refs = (gain_ref, bias_ref, w_in_ref, b_in_ref, w_out_ref, b_out_ref, scale_ref)
    grad_conv, branch, grad_in, grad_out, vec, bin_sum = dense_part(
        conv[...].reshape(256, C), late.reshape(256, C), dense_weights(refs)
    )
    gc_ref[0:2] = grad_conv[0:2]
    gc_ref[6:8] = grad_conv[2:4]
    branch_ref[0:2] = branch[0:2]
    branch_ref[6:8] = branch[2:4]
    pack[ROW_VEC : ROW_VEC + 4, 0:C] = vec + early_vec[...]
    bin_sum = bin_sum + early_bin[...]
    grad_in = grad_in + early_in[...]
    grad_out = grad_out + early_out[...]
    for j in range(3):
        lanes = slice(j * LANES, (j + 1) * LANES)
        pack[ROW_BIN + j : ROW_BIN + j + 1, :] = bin_sum[:, lanes]
        pack[ROW_IN + j * C : ROW_IN + (j + 1) * C, :] = grad_in[:, lanes]
        pack[ROW_OUT + j * C : ROW_OUT + (j + 1) * C, :] = grad_out[:, lanes]

    masks, low_back, high_back = row_masks(), row_masks(-low_y), row_masks(-high_y)
    for k, plane in enumerate((0, 1, 6, 7)):
        grads = [gc_ref[plane, x] for x in range(B)]
        move_rows(grads, moved, k, masks)
        move_rows(grads, moved_halo, k, low_back if k < 2 else high_back)

    def kernel_step(b, carry):
        def pairs(a):
            for k, plane in enumerate((0, 1, 6, 7)):
                held = dict(NEAR[plane]).get(a)
                if held is None:
                    grads = [moved[b, k, x] for x in range(B)]
                    yield grads, [source[plane + a - 2, x] for x in range(B)], True
                else:
                    grads = [moved_halo[b, k, x] for x in range(B)]
                    yield grads, [halo[held, 8 + j] for j in range(12)], False

        for a in range(T):
            row = a * T + b
            sums = kernel_taps(pairs(a))
            kernel_rows[row, 0:T, :] = jnp.concatenate(
                [
                    jnp.sum(sums[e] + early_rows[row, e], axis=0, keepdims=True)
                    for e in range(T)
                ],
                axis=0,
            )
        return carry

    lax.fori_loop(0, T, kernel_step, 0)
    for k in range(T * T):
        row = ROW_KERNEL + k * T
        pack[row : row + T, 0:C] = kernel_rows[k, 0:T, :]

    for d in range(parts):
        first = d * chunk
        rows = max(0, min(chunk, ROWS - first))
        if rows:
            packed_ref[d, 0:rows, :] = pack[first : first + rows, :].astype(BF16)
        if rows < chunk:
            packed_ref[d, rows:chunk, :] = jnp.zeros((chunk - rows, LANES), BF16)


def back_kernel(
    odd_ref,
    even_ref,
    source,
    taps,
    gc_ref,
    branch_ref,
    fluid_ref,
    gain_ref,
    bias_ref,
    w_in_ref,
    b_in_ref,
    w_out_ref,
    scale_ref,
    table_vmem,
    up_hbm,
    feat_hbm,
    out_ref,
    mixed_ref,
    table_ref,
    up_ref,
    feat_ref,
    sems,
    rims,
    rim_seeds,
    conv,
    halo,
):
    copies = start_copies(
        sems, (table_vmem, table_ref), (up_hbm, up_ref), (feat_hbm, feat_ref)
    )
    clear_halo(halo, 4)
    from_low, from_high = halo_planes(even_ref, odd_ref)
    for k in range(4):
        below, above = spread(from_low(k)), spread(from_high(k))
        for x in range(B):
            rims[k, x] = below[x]
            rims[4 + k, x] = above[x]
    for k in range(2):
        below, above = spread(from_low(4 + k)), spread(from_high(4 + k))
        for x in range(B):
            rim_seeds[k, x] = below[x]
            rim_seeds[2 + k, x] = above[x]
    copies[0].wait()
    own, low, high, live = layer_places(table_ref)
    low_x, low_y = offset(own, low)
    high_x, high_y = offset(own, high)
    for k in range(2):
        put_halo(halo, k, [source[k, x] for x in range(B)], -low_x)
        put_halo(halo, 2 + k, [source[6 + k, x] for x in range(B)], -high_x)
    masks, low_back, high_back = row_masks(), row_masks(-low_y), row_masks(-high_y)
    for k, (pairs, near, near_masks) in enumerate(
        (
            ([(0, 0), (1, 1), (2, 2), (3, 3)], [(4, 0)], low_back),
            ([(0, 1), (1, 2), (2, 3)], [(3, 0), (4, 1)], low_back),
            ([(2, 4), (3, 5), (4, 6)], [(0, 2), (1, 3)], high_back),
            ([(1, 4), (2, 5), (3, 6), (4, 7)], [(0, 3)], high_back),
        )
    ):
        out = conv_plane(rims, taps, pairs, masks, halo, near, near_masks)
        for x in range(B):
            conv[k, x] = out[x]
    refs = (gain_ref, bias_ref, w_in_ref, b_in_ref, w_out_ref, None, scale_ref)
    grad_conv = dense_part(
        conv[...].reshape(256, C), rim_seeds[...].reshape(256, C), dense_weights(refs), False
    )

    clear_halo(halo, 4)
    for k in range(2):
        put_halo(halo, k, [grad_conv[k, x] for x in range(B)], low_x)
        put_halo(halo, 2 + k, [grad_conv[2 + k, x] for x in range(B)], high_x)
    copies[1].wait()
    copies[2].wait()
    back_taps = Flipped(taps)
    scale_wide = gather_lanes([scale_ref[...]] * B)

    def finish(z, out):
        seed = up_ref[z].astype(F32) * live
        mask = fluid_ref[z].astype(F32) * live
        out_ref[z] = (seed + gather_lanes(out) * mask).astype(BF16)
        wide = gather_lanes([branch_ref[z, x] for x in range(B)])
        mixed_ref[z] = ((feat_ref[z].astype(F32) + scale_wide * wide) * live).astype(BF16)

    def middle_step(z, carry):
        finish(2 + z, middle_plane(gc_ref, back_taps, z, masks))
        return carry

    lax.fori_loop(0, 4, middle_step, 0)
    low_masks, high_masks = row_masks(low_y), row_masks(high_y)
    for z in (0, 1, 6, 7):
        near = low_masks if z < 2 else high_masks
        finish(z, conv_plane(gc_ref, back_taps, own_pairs(z), masks, halo, NEAR[z], near))


def reduce_kernel(parts, factor, got_ref, out_ref):
    def add(d, total):
        return total + got_ref[d].astype(F32)

    total = lax.fori_loop(0, parts, add, jnp.zeros(got_ref.shape[1:], F32), unroll=8)
    total = (total * factor).astype(BF16)

    def copy(d, carry):
        out_ref[d] = total
        return carry

    lax.fori_loop(0, parts, copy, 0, unroll=8)


def unpack_kernel(chunk, got_ref, kernel_ref, in_ref, out_ref, bin_ref, vec_ref, pack):
    for d in range(got_ref.shape[0]):
        first = d * chunk
        if first >= ROWS:
            break
        rows = min(chunk, ROWS - first)
        pack[first : first + rows, :] = got_ref[d, 0:rows, :].astype(F32)
    for j in range(3):
        lanes = slice(j * LANES, (j + 1) * LANES)
        in_ref[:, lanes] = pack[ROW_IN + j * C : ROW_IN + (j + 1) * C, :]
        out_ref[:, lanes] = pack[ROW_OUT + j * C : ROW_OUT + (j + 1) * C, :]
        bin_ref[lanes] = pack[ROW_BIN + j, :]
    vec_ref[...] = pack[ROW_VEC : ROW_VEC + 4, 0:C]
    for a in range(T):
        for b in range(T):
            row = ROW_KERNEL + (a * T + b) * T
            kernel_ref[a, b] = pack[row : row + T, 0:C]


def local(
    features,
    wall_mask,
    block_positions,
    dw_kernel,
    norm_gain,
    norm_bias,
    w_in,
    b_in,
    w_out,
    b_out,
    layer_scale,
    upstream,
):
    feat = features[0, 0, 0]
    walls = wall_mask[0, 0, 0]
    up = upstream[0, 0, 0]
    table = block_positions[0, :, 0]
    layers = lax.axis_size("space")
    parts = layers * lax.axis_size("sample")
    chunk = 8 * (-(-ROWS // (8 * parts)))
    block = (B, B, B * C)

    held = [pinned(array) for array in (table, feat, walls, up, dw_kernel)]
    for_even, for_odd, masked, fluid, dw = pl.pallas_call(
        send_kernel,
        out_shape=[
            jax.ShapeDtypeStruct((6, B, B * C), BF16),
            jax.ShapeDtypeStruct((6, B, B * C), BF16),
            jax.ShapeDtypeStruct(block, BF16),
            jax.ShapeDtypeStruct(block, BF16),
            jax.ShapeDtypeStruct((T, T, T, C), F32),
        ],
        in_specs=[hbm()] * 5,
        out_specs=[vmem()] * 5,
        scratch_shapes=[
            pltpu.SMEM((layers,), jnp.int32),
            pltpu.VMEM(block, BF16),
            pltpu.VMEM((B, B * B), jnp.int32),
            pltpu.VMEM(block, BF16),
            pltpu.SemaphoreType.DMA((5,)),
        ],
        compiler_params=params(),
        name="send",
    )(*held)

    def swap(array, first):
        pairs = [(i, i + 1) for i in range(first, layers - 1, 2)]
        return lax.ppermute(array, "space", pairs + [(j, i) for i, j in pairs])

    odd = swap(for_odd, 1)
    even = swap(for_even, 0)

    weights = [
        norm_gain.reshape(1, C),
        norm_bias.reshape(1, C),
        w_in,
        b_in,
        w_out.T,
        b_out.reshape(1, C),
        layer_scale.reshape(1, C),
    ]
    operands = [pinned(array) for array in [table, up] + weights]
    source, seeds, taps, conv, *held = pl.pallas_call(
        early_kernel,
        out_shape=[
            jax.ShapeDtypeStruct((B, B, B, C), F32),
            jax.ShapeDtypeStruct((B, B, B, C), F32),
            jax.ShapeDtypeStruct((T, T, T, B, C), F32),
            jax.ShapeDtypeStruct((B, B, B, C), F32),
        ]
        + [jax.ShapeDtypeStruct(array.shape, array.dtype) for array in weights]
        + [
            jax.ShapeDtypeStruct((4, B, B, C), F32),
            jax.ShapeDtypeStruct((4, B, B, C), F32),
            jax.ShapeDtypeStruct((C, HID), F32),
            jax.ShapeDtypeStruct((C, HID), F32),
            jax.ShapeDtypeStruct((4, C), F32),
            jax.ShapeDtypeStruct((1, HID), F32),
            jax.ShapeDtypeStruct((T * T, T, B, C), F32),
            jax.ShapeDtypeStruct((layers,), jnp.int32),
        ],
        in_specs=[vmem()] * 2 + [hbm()] * len(operands),
        out_specs=[vmem()] * (12 + len(weights)),
        scratch_shapes=[
            pltpu.SMEM((layers,), jnp.int32),
            pltpu.VMEM(block, BF16),
            pltpu.VMEM((T, 4, B, B, C), F32),
            pltpu.SemaphoreType.DMA((len(operands) + 1,)),
        ],
        compiler_params=params(),
        cost_estimate=pl.CostEstimate(flops=40_000_000, bytes_accessed=800_000, transcendentals=0),
        name="early",
    )(masked, dw, *operands)

    branch, grad_conv, packed = pl.pallas_call(
        functools.partial(main_kernel, chunk, parts),
        out_shape=[
            jax.ShapeDtypeStruct((B, B, B, C), F32),
            jax.ShapeDtypeStruct((B, B, B, C), F32),
            jax.ShapeDtypeStruct((parts, chunk, LANES), BF16),
        ],
        in_specs=[vmem()] * (6 + len(held)),
        out_specs=[vmem()] * 3,
        scratch_shapes=[
            pltpu.SMEM((layers,), jnp.int32),
            pltpu.SemaphoreType.DMA((1,)),
            pltpu.VMEM((4, 28, B, C), F32),
            pltpu.VMEM((4, B, B, C), F32),
            pltpu.VMEM((T, 4, B, B, C), F32),
            pltpu.VMEM((T, 4, B, B, C), F32),
            pltpu.VMEM((T * T, B, C), F32),
            pltpu.VMEM((ROWS, LANES), F32),
        ],
        compiler_params=params(),
        name="main",
    )(odd, even, source, seeds, taps, conv, *held)

    axes = ("space", "sample")
    scattered = lax.all_to_all(packed, axes, 0, 0, tiled=True)

    weights = held[:5] + held[6:7]
    grad_field, mixed = pl.pallas_call(
        back_kernel,
        out_shape=[jax.ShapeDtypeStruct(block, BF16)] * 2,
        in_specs=[vmem()] * (8 + len(weights)) + [hbm()] * 2,
        out_specs=[vmem()] * 2,
        scratch_shapes=[
            pltpu.SMEM((layers,), jnp.int32),
            pltpu.VMEM(block, BF16),
            pltpu.VMEM(block, BF16),
            pltpu.SemaphoreType.DMA((3,)),
            pltpu.VMEM((8, B, B, C), F32),
            pltpu.VMEM((4, B, B, C), F32),
            pltpu.VMEM((4, B, B, C), F32),
            pltpu.VMEM((4, 28, B, C), F32),
        ],
        compiler_params=params(),
        cost_estimate=pl.CostEstimate(flops=60_000_000, bytes_accessed=800_000, transcendentals=0),
        name="back",
    )(
        odd,
        even,
        source,
        taps,
        grad_conv,
        branch,
        fluid,
        *weights,
        held[-1],
        *[pinned(array) for array in (up, feat)],
    )

    factor = 1.0 / math.sqrt(parts * B**3)
    summed = pl.pallas_call(
        functools.partial(reduce_kernel, parts, factor),
        out_shape=jax.ShapeDtypeStruct((parts, chunk, LANES), BF16),
        in_specs=[vmem()],
        out_specs=vmem(),
        compiler_params=params(),
        name="reduce",
    )(scattered)
    gathered = lax.all_to_all(summed, axes, 0, 0, tiled=True)
    grad_kernel, grad_w_in, grad_w_out, grad_b_in, grad_vectors = pl.pallas_call(
        functools.partial(unpack_kernel, chunk),
        out_shape=[
            jax.ShapeDtypeStruct((T, T, T, C), F32),
            jax.ShapeDtypeStruct((C, HID), F32),
            jax.ShapeDtypeStruct((C, HID), F32),
            jax.ShapeDtypeStruct((HID,), F32),
            jax.ShapeDtypeStruct((4, C), F32),
        ],
        in_specs=[vmem()],
        out_specs=[vmem()] * 5,
        scratch_shapes=[pltpu.VMEM((ROWS, LANES), F32)],
        compiler_params=params(),
        name="unpack",
    )(gathered)
    lead = (1, 1, 1)
    return (
        mixed.reshape(lead + block),
        grad_field.reshape(lead + block),
        grad_kernel,
        grad_w_in,
        grad_w_out.T,
        grad_b_in,
        grad_vectors,
    )


def solution(mesh):
    return jax.shard_map(
        local,
        mesh=mesh,
        in_specs=(
            P("sample", "space", None, None, None, None),
            P("sample", "space", None, None, None),
            P("sample", None, None),
            P(),
            P(),
            P(),
            P(),
            P(),
            P(),
            P(),
            P(),
            P("sample", "space", None, None, None, None),
        ),
        out_specs=(
            P("sample", "space", None, None, None, None),
            P("sample", "space", None, None, None, None),
            P(),
            P(),
            P(),
            P(),
            P(),
        ),
        check_vma=False,
    )
```

time: 273 us -> 42.1 us (0.15)
  waiting for transfers between devices: 112 us -> 3.63 us
  other arithmetic: 48.8 us -> 0 us
  blocking collectives: 43.1 us -> 14.8 us
  local copies, waits for them, and re-layouts: 26.8 us -> 0 us
  between operations: 26.5 us -> 0.7 us
  Pallas kernels: 0 us -> 15.1 us
  matrix products: 3.79 us -> 0 us
    psum x1 -> x0, waiting for transfers between devices: 109 us -> none  [local(): lax.psum((local_parts[0], local_parts[1], local_parts[2], local_parts[3],...]
    psum x1 -> x0, blocking collectives: 43.1 us -> none  [local(): lax.psum((local_parts[0], local_parts[1], local_parts[2], local_parts[3],...]
    broadcast_in_dim x1 -> x0, other arithmetic: 15.2 us -> none  [local(): grad_field[None, None]]
    pallas_call x0 -> x6, Pallas kernels: none -> 15.1 us  [the longest x1 5.6 us: local(): pl.pallas_call(back_kernel, out_shape=[jax.ShapeDtypeStruct(block, BF16)]...]
    all_to_all x0 -> x1, blocking collectives: none -> 14.8 us  [local(): scattered = lax.all_to_all(packed, axes, 0, 0, tiled=True)]
    add x1 -> x0, other arithmetic: 13.9 us -> none  [depthwise(): running = running + window.astype(jnp.float32) * weight_row]
    reduce_sum x142 -> x0, other arithmetic: 13.4 us -> none  [the longest x15 10.4 us: kernel_grad(): per_lane = jnp.sum(window.astype(jnp.float32) * grad_wide, axis=(0, 1, 2))]
    mul x127 -> x0, local copies, waits for them, and re-layouts: 9.72 us -> none  [the longest x125 9.46 us: depthwise(): running = running + window.astype(jnp.float32) * weight_row]
  transfers between devices with their start and end apart: 5 -> 3, of which waited for: 2 -> 1; matrix products, arithmetic and copies ran while one was open for 11% -> 0% of each run, Pallas kernels for 0% -> 23%
where the time goes in v1:
time: 42.1 us; the launch traced here: 41.9 us
  Pallas kernels  15.1 us (36%)
  blocking collectives  14.8 us (35%)
  starting transfers between devices  7.6 us (18%)
  waiting for transfers between devices  3.63 us (9%)
  between operations  0.7 us (2%)
    all_to_all x1, blocking collectives, local(): scattered = lax.all_to_all(packed, axes, 0, 0, tiled=True)  14.8 us
    pallas_call x1, Pallas kernels, local(): pl.pallas_call(back_kernel, out_shape=[jax.ShapeDtypeStruct(block, BF16)]...  5.6 us
    ppermute x2, starting transfers between devices, swap(): return lax.ppermute(array, 'space', pairs + [(j, i) for i, j in pairs])  5.23 us
    pallas_call x1, Pallas kernels, local(): pl.pallas_call(early_kernel, out_shape=[jax.ShapeDtypeStruct((B, B, B, C)...  3.92 us
    all_to_all x1, waiting for transfers between devices, local(): gathered = lax.all_to_all(summed, axes, 0, 0, tiled=True)  3.62 us
    pallas_call x1, Pallas kernels, local(): pl.pallas_call(functools.partial(main_kernel, chunk, parts), out_shape=[j...  3.03 us
    all_to_all x1, starting transfers between devices, local(): gathered = lax.all_to_all(summed, axes, 0, 0, tiled=True)  2.37 us
    pallas_call x1, Pallas kernels, local(): pl.pallas_call(send_kernel, out_shape=[jax.ShapeDtypeStruct((6, B, B * C)...  1.07 us
  transfers between devices with their start and end apart: 3, of which 1 were waited for; matrix products, arithmetic and copies ran while one was open for 0% of the time, Pallas kernels for 23%

profile of v1, /device:TPU:1, one launch (start us, length us, event | category | flops | bytes accessed | tf_op | source)
XLA Modules:
  0.0 41.9 jit_solution(10355750269018838291)
XLA Ops:
  0.6 1.1 %send.1 = (bf16[6,8,768]{2,1,0:T(8,128)(2,1)S(1)}, bf16[6,8,768]{2,1,0:T(8,128)(2,1)S(1)}, bf16[8,8,768]{2,1,0:T(8,128)(2,1)S(1)}, bf16[8,8,768]{2,1,0:T(8,128)(2,1)S(1)}, f32[5,5,5,96]{3,2,1,0:T(8,128)S(1)}) custom-call(s32[16]{0:T(128)} %bitcast.19, bf16[8,8,768]{2,1,0:T(8,128)(2,1)} %bitcast.15, s32[8,64]{1,0:T(8,128)} %bitcast.18, ...), custom_call_target="tpu_custom_call" | custom-call | tf_op jit(solution)/shard_map/send/pallas_call | solution.py:736
  1.7 0.7 %collective-permute-start = (bf16[6,8,768]{2,1,0:T(8,128)(2,1)S(1)}, bf16[6,8,768]{2,1,0:T(8,128)(2,1)S(1)}, u32[]{:S(2)}, u32[]{:S(2)}) collective-permute-start(bf16[6,8,768]{2,1,0:T(8,128)(2,1)S(1)} %get-tuple-element.41), channel_id=1, source_target_pairs={{2,4},{6,8},{10,12},{14,16},{18,20},{22,24},{26,28},{4,2},{8,6},{1... | collective-permute-start | bytes 221192 | tf_op jit(solution)/shard_map/ppermute | solution.py:760
  2.4 4.6 %collective-permute-start.1 = (bf16[6,8,768]{2,1,0:T(8,128)(2,1)S(1)}, bf16[6,8,768]{2,1,0:T(8,128)(2,1)S(1)}, u32[]{:S(2)}, u32[]{:S(2)}) collective-permute-start(bf16[6,8,768]{2,1,0:T(8,128)(2,1)S(1)} %get-tuple-element.42), channel_id=1, source_target_pairs={{0,2},{4,6},{8,10},{12,14},{16,18},{20,22},{24,26},{28,30},{2,0},{... | collective-permute-start | bytes 221192 | tf_op jit(solution)/shard_map/ppermute | solution.py:760
  6.9 3.9 %early.1 = (f32[8,8,8,96]{3,2,1,0:T(8,128)S(1)}, f32[8,8,8,96]{3,2,1,0:T(8,128)S(1)}, f32[5,5,5,8,96]{4,3,2,1,0:T(8,128)S(1)}, f32[8,8,8,96]{3,2,1,0:T(8,128)S(1...) custom-call(bf16[8,8,768]{2,1,0:T(8,128)(2,1)S(1)} %get-tuple-elemen, ...), custom_call_target="tpu_custom_call" | custom-call | flops 40000000 | bytes 800000 | tf_op jit(solution)/shard_map/early/pallas_call | solution.py:775
  10.9 0.0 collective-permute-done.odd_ref
  10.9 0.0 collective-permute-done.1.even_ref
  10.9 3.0 %main.1 = (f32[8,8,8,96]{3,2,1,0:T(8,128)S(1)}, f32[8,8,8,96]{3,2,1,0:T(8,128)S(1)}, bf16[32,24,128]{2,1,0:T(8,128)(2,1)S(1)}) custom-call(bf16[6,8,768]{2,1,0:T(8,128)(2,1)S(1)} %collective-permute-done.odd_ref, bf16[6,8,768]{2,1,0:T(8,128)(2,1)S(1)} %collective-permute-done.1.even_ref, f32[8,8,8,96]{3,2,1,0:T(8,128)S(1)} %get-tuple-element.45.source, ...), custom_call_target="tpu_custom_call" | custom-call | tf_op jit(solution)/shard_map/main/pallas_call | solution.py:807
  13.9 14.8 %all_to_all.10.got_ref = bf16[32,24,128]{2,1,0:T(8,128)(2,1)S(1)} all-to-all(bf16[32,24,128]{2,1,0:T(8,128)(2,1)S(1)} %get-tuple-element.69), channel_id=1, replica_groups=mesh['space'=16,'sample'=2] {'space','sample'}, dimensions={0} | all-to-all | bytes 393216 | tf_op jit(solution)/shard_map/all_to_all | solution.py:831
  28.8 0.7 %reduce.1 = bf16[32,24,128]{2,1,0:T(8,128)(2,1)} custom-call(bf16[32,24,128]{2,1,0:T(8,128)(2,1)S(1)} %all_to_all.10.got_ref), custom_call_target="tpu_custom_call" | custom-call | tf_op jit(solution)/shard_map/reduce/pallas_call | solution.py:866
  29.5 2.4 %all-to-all-start.1 = ((bf16[32,24,128]{2,1,0:T(8,128)(2,1)}), bf16[32,24,128]{2,1,0:T(8,128)(2,1)S(1)}, u32[]{:S(2)}, u32[]{:S(2)}) async-start(bf16[32,24,128]{2,1,0:T(8,128)(2,1)} %reduce.1), calls=%async_computation.1 | async-start | bytes 393216 | tf_op jit(solution)/shard_map/all_to_all | solution.py:874
  31.9 5.6 %back.1 = (bf16[8,8,768]{2,1,0:T(8,128)(2,1)}, bf16[8,8,768]{2,1,0:T(8,128)(2,1)}) custom-call(bf16[6,8,768]{2,1,0:T(8,128)(2,1)S(1)} %collective-permute-done.odd_ref, bf16[6,8,768]{2,1,0:T(8,128)(2,1)S(1)} %collective-permute-done.1.even_ref, f32[8,8,8,96]{3,2,1,0:T(8,128)S(1)} %get-tuple-element.45.source, ...), custom_call_target="tpu_custom_call" | custom-call | flops 60000000 | bytes 800000 | tf_op jit(solution)/shard_map/back/pallas_call | solution.py:834
  37.5 3.6 %all-to-all-done.1.got_ref = bf16[32,24,128]{2,1,0:T(8,128)(2,1)S(1)} async-done(((bf16[32,24,128]{2,1,0:T(8,128)(2,1)}), bf16[32,24,128]{2,1,0:T(8,128)(2,1)S(1)}, u32[]{:S(2)}, u32[]{:S(2)}) %all-to-all-start.1) | async-done | bytes 196640 | tf_op jit(solution)/shard_map/all_to_all | solution.py:874
  41.1 0.8 %unpack.1 = (f32[5,5,5,96]{3,2,1,0:T(8,128)}, f32[96,384]{1,0:T(8,128)}, f32[96,384]{1,0:T(8,128)}, f32[384]{0:T(512)}, f32[4,96]{1,0:T(4,128)}) custom-call(bf16[32,24,128]{2,1,0:T(8,128)(2,1)S(1)} %all-to-all-done.1.got_ref), custom_call_target="tpu_custom_call" | custom-call | tf_op jit(solution)/shard_map/unpack/pallas_call | solution.py:875
Async XLA Ops:
  1.7 9.2 %collective-permute-start = (bf16[6,8,768]{2,1,0:T(8,128)(2,1)S(1)}, bf16[6,8,768]{2,1,0:T(8,128)(2,1)S(1)}, u32[]{:S(2)}, u32[]{:S(2)}) collective-permute-start(bf16[6,8,768]{2,1,0:T(8,128)(2,1)S(1)} %get-tuple-element.41), channel_id=1, source_target_pairs={{2,4},{6,8},{10,12},{14,16},{18,20},{22,24},{26,28},{4,2},{8,6},{1... | collective-permute-start | bytes 221192 | tf_op jit(solution)/shard_map/ppermute | solution.py:760
  2.4 8.5 %collective-permute-start.1 = (bf16[6,8,768]{2,1,0:T(8,128)(2,1)S(1)}, bf16[6,8,768]{2,1,0:T(8,128)(2,1)S(1)}, u32[]{:S(2)}, u32[]{:S(2)}) collective-permute-start(bf16[6,8,768]{2,1,0:T(8,128)(2,1)S(1)} %get-tuple-element.42), channel_id=1, source_target_pairs={{0,2},{4,6},{8,10},{12,14},{16,18},{20,22},{24,26},{28,30},{2,0},{... | collective-permute-start | bytes 221192 | tf_op jit(solution)/shard_map/ppermute | solution.py:760
  29.5 11.6 %all-to-all-start.1 = ((bf16[32,24,128]{2,1,0:T(8,128)(2,1)}), bf16[32,24,128]{2,1,0:T(8,128)(2,1)S(1)}, u32[]{:S(2)}, u32[]{:S(2)}) async-start(bf16[32,24,128]{2,1,0:T(8,128)(2,1)} %reduce.1), calls=%async_computation.1 | async-start | bytes 393216 | tf_op jit(solution)/shard_map/all_to_all | solution.py:874

commit v2 on v1

--- a/solution.py
+++ b/solution.py
@@ -209,22 +209,13 @@
             acc[x] = acc[x] + window[x + e] * weight
 
 
-def row_masks(start=None):
-    masks = []
-    for by in range(-2, 3):
-        row = rows_of() + by if start is None else rows_of() + (by - start)
-        inside = (row >= 0) & (row < B)
-        masks.append(None if start is None and by == 0 else jnp.where(inside, 1.0, 0.0))
-    return masks
-
-
-def shift_rows(value, by, masks):
+def shift_rows(value, by, start):
+    row = rows_of() + (by - start)
     rolled = value if by == 0 else pltpu.roll(value, (-by) % B, 0)
-    mask = masks[by + 2]
-    return rolled if mask is None else rolled * mask
-
-
-def conv_plane(source, taps, own, masks, halo=None, halos=(), halo_masks=None):
+    return jnp.where((row >= 0) & (row < B), rolled, 0.0)
+
+
+def conv_plane(source, taps, own, halo=None, halos=(), start=0):
     out = [jnp.zeros((B, C), F32) for _ in range(B)]
     for b in range(T):
         if own:
@@ -232,18 +223,18 @@
             for a, plane in own:
                 add_own(acc, [source[plane, x] for x in range(B)], taps, a, b)
             for x in range(B):
-                out[x] = out[x] + shift_rows(acc[x], b - 2, masks)
+                out[x] = out[x] + shift_rows(acc[x], b - 2, 0)
         if halos:
             acc = [jnp.zeros((B, C), F32) for _ in range(B)]
             for a, plane in halos:
                 add_halo(acc, [halo[plane, 8 + j] for j in range(12)], taps, a, b)
             for x in range(B):
-                out[x] = out[x] + shift_rows(acc[x], b - 2, halo_masks)
+                out[x] = out[x] + shift_rows(acc[x], b - 2, start)
     return out
 
 
-def middle_plane(source, taps, first, masks):
-    return conv_plane(source, taps, [(a, first + a) for a in range(T)], masks)
+def middle_plane(source, taps, first):
+    return conv_plane(source, taps, [(a, first + a) for a in range(T)])
 
 
 OWN_TAPS = {0: (2, 3, 4), 1: (1, 2, 3, 4), 6: (0, 1, 2, 3), 7: (0, 1, 2)}
@@ -332,13 +323,15 @@
                 else:
                     value = window[x + e]
                 acc[e][x & 1] = acc[e][x & 1] + value * grads[x]
-    return [pair[0] + pair[1] for pair in acc]
-
-
-def move_rows(grads, moved, k, masks):
+    return jnp.concatenate(
+        [jnp.sum(pair[0] + pair[1], axis=0, keepdims=True) for pair in acc], axis=0
+    )
+
+
+def move_rows(grads, moved, k):
     for x in range(B):
         for b in range(T):
-            moved[b, k, x] = shift_rows(grads[x], 2 - b, masks)
+            moved[b, k, x] = shift_rows(grads[x], 2 - b, 0)
 
 
 def early_kernel(
@@ -399,10 +392,9 @@
 
     lax.fori_loop(0, B, own_planes, 0, unroll=True)
     wide_taps(dw_ref, taps)
-    masks = row_masks()
 
     def middle_step(z, carry):
-        out = middle_plane(source, taps, z, masks)
+        out = middle_plane(source, taps, z)
         for x in range(B):
             conv[2 + z, x] = out[x]
         return carry
@@ -410,7 +402,7 @@
     lax.fori_loop(0, 4, middle_step, 0)
 
     def edge(plane):
-        out = conv_plane(source, taps, own_pairs(plane), masks)
+        out = conv_plane(source, taps, own_pairs(plane))
         for x in range(B):
             conv[plane, x] = out[x]
 
@@ -439,11 +431,11 @@
     bin_ref[...] = bin_sum
 
     for k in range(4):
-        move_rows([gc_ref[k, x] for x in range(B)], moved, k, masks)
+        move_rows([gc_ref[k, x] for x in range(B)], moved, k)
 
     def kernel_step(b, carry):
         for a in range(T):
-            sums = kernel_taps(
+            rows_ref[a * T + b, 0:T, :] = kernel_taps(
                 (
                     [moved[b, k, x] for x in range(B)],
                     [source[k + a, x] for x in range(B)],
@@ -451,8 +443,6 @@
                 )
                 for k in range(4)
             )
-            for e in range(T):
-                rows_ref[a * T + b, e] = sums[e]
         return carry
 
     lax.fori_loop(0, T, kernel_step, 0)
@@ -513,10 +503,8 @@
     for k in range(2):
         put_halo(halo, k, below[k], low_x)
         put_halo(halo, 2 + k, above[k], high_x)
-    low_masks, high_masks = row_masks(low_y), row_masks(high_y)
     for k, plane in enumerate((0, 1, 6, 7)):
-        near = low_masks if k < 2 else high_masks
-        out = conv_plane(source, taps, [], None, halo, NEAR[plane], near)
+        out = conv_plane(source, taps, [], halo, NEAR[plane], low_y if k < 2 else high_y)
         for x in range(B):
             conv[k, x] = conv_ref[plane, x] + out[x]
 
@@ -539,11 +527,13 @@
         pack[ROW_IN + j * C : ROW_IN + (j + 1) * C, :] = grad_in[:, lanes]
         pack[ROW_OUT + j * C : ROW_OUT + (j + 1) * C, :] = grad_out[:, lanes]
 
-    masks, low_back, high_back = row_masks(), row_masks(-low_y), row_masks(-high_y)
     for k, plane in enumerate((0, 1, 6, 7)):
         grads = [gc_ref[plane, x] for x in range(B)]
-        move_rows(grads, moved, k, masks)
-        move_rows(grads, moved_halo, k, low_back if k < 2 else high_back)
+        move_rows(grads, moved, k)
+        start = low_y if k < 2 else high_y
+        for x in range(B):
+            for b in range(T):
+                moved_halo[b, k, x] = shift_rows(grads[x], 2 - b, -start)
 
     def kernel_step(b, carry):
         def pairs(a):
@@ -558,14 +548,7 @@
 
         for a in range(T):
             row = a * T + b
-            sums = kernel_taps(pairs(a))
-            kernel_rows[row, 0:T, :] = jnp.concatenate(
-                [
-                    jnp.sum(sums[e] + early_rows[row, e], axis=0, keepdims=True)
-                    for e in range(T)
-                ],
-                axis=0,
-            )
+            kernel_rows[row, 0:T, :] = early_rows[row, 0:T, :] + kernel_taps(pairs(a))
         return carry
 
     lax.fori_loop(0, T, kernel_step, 0)
@@ -632,16 +615,15 @@
     for k in range(2):
         put_halo(halo, k, [source[k, x] for x in range(B)], -low_x)
         put_halo(halo, 2 + k, [source[6 + k, x] for x in range(B)], -high_x)
-    masks, low_back, high_back = row_masks(), row_masks(-low_y), row_masks(-high_y)
-    for k, (pairs, near, near_masks) in enumerate(
+    for k, (pairs, near, start) in enumerate(
         (
-            ([(0, 0), (1, 1), (2, 2), (3, 3)], [(4, 0)], low_back),
-            ([(0, 1), (1, 2), (2, 3)], [(3, 0), (4, 1)], low_back),
-            ([(2, 4), (3, 5), (4, 6)], [(0, 2), (1, 3)], high_back),
-            ([(1, 4), (2, 5), (3, 6), (4, 7)], [(0, 3)], high_back),
+            ([(0, 0), (1, 1), (2, 2), (3, 3)], [(4, 0)], -low_y),
+            ([(0, 1), (1, 2), (2, 3)], [(3, 0), (4, 1)], -low_y),
+            ([(2, 4), (3, 5), (4, 6)], [(0, 2), (1, 3)], -high_y),
+            ([(1, 4), (2, 5), (3, 6), (4, 7)], [(0, 3)], -high_y),
         )
     ):
-        out = conv_plane(rims, taps, pairs, masks, halo, near, near_masks)
+        out = conv_plane(rims, taps, pairs, halo, near, start)
         for x in range(B):
             conv[k, x] = out[x]
     refs = (gain_ref, bias_ref, w_in_ref, b_in_ref, w_out_ref, None, scale_ref)
@@ -666,17 +648,16 @@
         mixed_ref[z] = ((feat_ref[z].astype(F32) + scale_wide * wide) * live).astype(BF16)
 
     def middle_step(z, carry):
-        finish(2 + z, middle_plane(gc_ref, back_taps, z, masks))
+        finish(2 + z, middle_plane(gc_ref, back_taps, z))
         return carry
 
     lax.fori_loop(0, 4, middle_step, 0)
-    low_masks, high_masks = row_masks(low_y), row_masks(high_y)
     for z in (0, 1, 6, 7):
-        near = low_masks if z < 2 else high_masks
-        finish(z, conv_plane(gc_ref, back_taps, own_pairs(z), masks, halo, NEAR[z], near))
-
-
-def reduce_kernel(parts, factor, got_ref, out_ref):
+        start = low_y if z < 2 else high_y
+        finish(z, conv_plane(gc_ref, back_taps, own_pairs(z), halo, NEAR[z], start))
+
+
+def reduce_kernel(parts, factor, got_ref, after_ref, out_ref):
     def add(d, total):
         return total + got_ref[d].astype(F32)
 
@@ -788,7 +769,7 @@
             jax.ShapeDtypeStruct((C, HID), F32),
             jax.ShapeDtypeStruct((4, C), F32),
             jax.ShapeDtypeStruct((1, HID), F32),
-            jax.ShapeDtypeStruct((T * T, T, B, C), F32),
+            jax.ShapeDtypeStruct((T * T, B, C), F32),
             jax.ShapeDtypeStruct((layers,), jnp.int32),
         ],
         in_specs=[vmem()] * 2 + [hbm()] * len(operands),
@@ -866,11 +847,11 @@
     summed = pl.pallas_call(
         functools.partial(reduce_kernel, parts, factor),
         out_shape=jax.ShapeDtypeStruct((parts, chunk, LANES), BF16),
-        in_specs=[vmem()],
+        in_specs=[vmem(), pl.BlockSpec(memory_space=pl.ANY)],
         out_specs=vmem(),
         compiler_params=params(),
         name="reduce",
-    )(scattered)
+    )(scattered, pinned(grad_field))
     gathered = lax.all_to_all(summed, axes, 0, 0, tiled=True)
     grad_kernel, grad_w_in, grad_w_out, grad_b_in, grad_vectors = pl.pallas_call(
         functools.partial(unpack_kernel, chunk),

time: 42.1 us -> 42.2 us (level)
  blocking collectives: 14.8 us -> 11.4 us
  starting transfers between devices: 7.6 us -> 11 us
    all_to_all x1, starting transfers between devices: 2.37 us -> 5.82 us  [local(): scattered = lax.all_to_all(packed, axes, 0, 0, tiled=True)]
    all_to_all x1, blocking collectives: 14.8 us -> 11.4 us  [local(): gathered = lax.all_to_all(summed, axes, 0, 0, tiled=True)]
    pallas_call x1, Pallas kernels: 0.73 us -> 0.07 us  [local(): pl.pallas_call(functools.partial(reduce_kernel, parts, factor), out_shape...]
    pallas_call x1, Pallas kernels: 3.03 us -> 3.67 us  [local(): pl.pallas_call(functools.partial(main_kernel, chunk, parts), out_shape=[j...]
where the time goes in v2:
time: 42.2 us; the launch traced here: 41.9 us
  Pallas kernels  15.1 us (36%)
  blocking collectives  11.4 us (27%)
  starting transfers between devices  11 us (26%)
  waiting for transfers between devices  3.68 us (9%)
  between operations  0.7 us (2%)
    all_to_all x1, blocking collectives, local(): gathered = lax.all_to_all(summed, axes, 0, 0, tiled=True)  11.4 us
    all_to_all x1, starting transfers between devices, local(): scattered = lax.all_to_all(packed, axes, 0, 0, tiled=True)  5.82 us
    pallas_call x1, Pallas kernels, local(): pl.pallas_call(back_kernel, out_shape=[jax.ShapeDtypeStruct(block, BF16)]...  5.55 us
    ppermute x2, starting transfers between devices, swap(): return lax.ppermute(array, 'space', pairs + [(j, i) for i, j in pairs])  5.23 us
    pallas_call x1, Pallas kernels, local(): pl.pallas_call(early_kernel, out_shape=[jax.ShapeDtypeStruct((B, B, B, C)...  3.96 us
    all_to_all x1, waiting for transfers between devices, local(): scattered = lax.all_to_all(packed, axes, 0, 0, tiled=True)  3.68 us
    pallas_call x1, Pallas kernels, local(): pl.pallas_call(functools.partial(main_kernel, chunk, parts), out_shape=[j...  3.67 us
    pallas_call x1, Pallas kernels, local(): pl.pallas_call(send_kernel, out_shape=[jax.ShapeDtypeStruct((6, B, B * C)...  1.07 us
  transfers between devices with their start and end apart: 3, of which 1 were waited for; matrix products, arithmetic and copies ran while one was open for 0% of the time, Pallas kernels for 23%

profile of v2, /device:TPU:1, one launch (start us, length us, event | category | flops | bytes accessed | tf_op | source)
XLA Modules:
  0.0 41.9 jit_solution(11623245700291748352)
XLA Ops:
  0.6 1.1 %send.1 = (bf16[6,8,768]{2,1,0:T(8,128)(2,1)S(1)}, bf16[6,8,768]{2,1,0:T(8,128)(2,1)S(1)}, bf16[8,8,768]{2,1,0:T(8,128)(2,1)S(1)}, bf16[8,8,768]{2,1,0:T(8,128)(2,1)S(1)}, f32[5,5,5,96]{3,2,1,0:T(8,128)S(1)}) custom-call(s32[16]{0:T(128)} %bitcast.20, bf16[8,8,768]{2,1,0:T(8,128)(2,1)} %bitcast.15, s32[8,64]{1,0:T(8,128)} %bitcast.19, ...), custom_call_target="tpu_custom_call" | custom-call | tf_op jit(solution)/shard_map/send/pallas_call | solution.py:717
  1.7 0.7 %collective-permute-start = (bf16[6,8,768]{2,1,0:T(8,128)(2,1)S(1)}, bf16[6,8,768]{2,1,0:T(8,128)(2,1)S(1)}, u32[]{:S(2)}, u32[]{:S(2)}) collective-permute-start(bf16[6,8,768]{2,1,0:T(8,128)(2,1)S(1)} %get-tuple-element.41), channel_id=1, source_target_pairs={{2,4},{6,8},{10,12},{14,16},{18,20},{22,24},{26,28},{4,2},{8,6},{1... | collective-permute-start | bytes 221192 | tf_op jit(solution)/shard_map/ppermute | solution.py:741
  2.4 4.6 %collective-permute-start.1 = (bf16[6,8,768]{2,1,0:T(8,128)(2,1)S(1)}, bf16[6,8,768]{2,1,0:T(8,128)(2,1)S(1)}, u32[]{:S(2)}, u32[]{:S(2)}) collective-permute-start(bf16[6,8,768]{2,1,0:T(8,128)(2,1)S(1)} %get-tuple-element.42), channel_id=1, source_target_pairs={{0,2},{4,6},{8,10},{12,14},{16,18},{20,22},{24,26},{28,30},{2,0},{... | collective-permute-start | bytes 221192 | tf_op jit(solution)/shard_map/ppermute | solution.py:741
  6.9 4.0 %early.1 = (f32[8,8,8,96]{3,2,1,0:T(8,128)S(1)}, f32[8,8,8,96]{3,2,1,0:T(8,128)S(1)}, f32[5,5,5,8,96]{4,3,2,1,0:T(8,128)S(1)}, f32[8,8,8,96]{3,2,1,0:T(8,128)S(1...) custom-call(bf16[8,8,768]{2,1,0:T(8,128)(2,1)S(1)} %get-tuple-elemen, ...), custom_call_target="tpu_custom_call" | custom-call | flops 40000000 | bytes 800000 | tf_op jit(solution)/shard_map/early/pallas_call | solution.py:756
  10.9 0.0 collective-permute-done.odd_ref
  10.9 0.0 collective-permute-done.1.even_ref
  10.9 3.7 %main.1 = (f32[8,8,8,96]{3,2,1,0:T(8,128)S(1)}, f32[8,8,8,96]{3,2,1,0:T(8,128)S(1)}, bf16[32,24,128]{2,1,0:T(8,128)(2,1)}) custom-call(bf16[6,8,768]{2,1,0:T(8,128)(2,1)S(1)} %collective-permute-done.odd_ref, bf16[6,8,768]{2,1,0:T(8,128)(2,1)S(1)} %collective-permute-done.1.even_ref, f32[8,8,8,96]{3,2,1,0:T(8,128)S(1)} %get-tuple-element.45.source, ...), custom_call_target="tpu_custom_call" | custom-call | tf_op jit(solution)/shard_map/main/pallas_call | solution.py:788
  14.6 5.8 %all-to-all-start = ((bf16[32,24,128]{2,1,0:T(8,128)(2,1)}), bf16[32,24,128]{2,1,0:T(8,128)(2,1)S(1)}, u32[]{:S(2)}, u32[]{:S(2)}) async-start(bf16[32,24,128]{2,1,0:T(8,128)(2,1)} %get-tuple-element.69), calls=%async_computation | async-start | bytes 393216 | tf_op jit(solution)/shard_map/all_to_all | solution.py:812
  20.4 5.5 %back.1 = (bf16[8,8,768]{2,1,0:T(8,128)(2,1)}, bf16[8,8,768]{2,1,0:T(8,128)(2,1)}) custom-call(bf16[6,8,768]{2,1,0:T(8,128)(2,1)S(1)} %collective-permute-done.odd_ref, bf16[6,8,768]{2,1,0:T(8,128)(2,1)S(1)} %collective-permute-done.1.even_ref, f32[8,8,8,96]{3,2,1,0:T(8,128)S(1)} %get-tuple-element.45.source, ...), custom_call_target="tpu_custom_call" | custom-call | flops 60000000 | bytes 800000 | tf_op jit(solution)/shard_map/back/pallas_call | solution.py:815
  26.0 3.7 %all-to-all-done.got_ref = bf16[32,24,128]{2,1,0:T(8,128)(2,1)S(1)} async-done(((bf16[32,24,128]{2,1,0:T(8,128)(2,1)}), bf16[32,24,128]{2,1,0:T(8,128)(2,1)S(1)}, u32[]{:S(2)}, u32[]{:S(2)}) %all-to-all-start) | async-done | bytes 196640 | tf_op jit(solution)/shard_map/all_to_all | solution.py:812
  29.7 0.1 reduce.1
  29.8 11.4 %all_to_all.10.got_ref = bf16[32,24,128]{2,1,0:T(8,128)(2,1)S(1)} all-to-all(bf16[32,24,128]{2,1,0:T(8,128)(2,1)S(1)} %reduce.1), channel_id=1, replica_groups=mesh['space'=16,'sample'=2] {'space','sample'}, dimensions={0} | all-to-all | bytes 393216 | tf_op jit(solution)/shard_map/all_to_all | solution.py:855
  41.2 0.8 %unpack.1 = (f32[5,5,5,96]{3,2,1,0:T(8,128)}, f32[96,384]{1,0:T(8,128)}, f32[96,384]{1,0:T(8,128)}, f32[384]{0:T(512)}, f32[4,96]{1,0:T(4,128)}) custom-call(bf16[32,24,128]{2,1,0:T(8,128)(2,1)S(1)} %all_to_all.10.got_ref), custom_call_target="tpu_custom_call" | custom-call | tf_op jit(solution)/shard_map/unpack/pallas_call | solution.py:856
Async XLA Ops:
  1.7 9.2 %collective-permute-start = (bf16[6,8,768]{2,1,0:T(8,128)(2,1)S(1)}, bf16[6,8,768]{2,1,0:T(8,128)(2,1)S(1)}, u32[]{:S(2)}, u32[]{:S(2)}) collective-permute-start(bf16[6,8,768]{2,1,0:T(8,128)(2,1)S(1)} %get-tuple-element.41), channel_id=1, source_target_pairs={{2,4},{6,8},{10,12},{14,16},{18,20},{22,24},{26,28},{4,2},{8,6},{1... | collective-permute-start | bytes 221192 | tf_op jit(solution)/shard_map/ppermute | solution.py:741
  2.4 8.5 %collective-permute-start.1 = (bf16[6,8,768]{2,1,0:T(8,128)(2,1)S(1)}, bf16[6,8,768]{2,1,0:T(8,128)(2,1)S(1)}, u32[]{:S(2)}, u32[]{:S(2)}) collective-permute-start(bf16[6,8,768]{2,1,0:T(8,128)(2,1)S(1)} %get-tuple-element.42), channel_id=1, source_target_pairs={{0,2},{4,6},{8,10},{12,14},{16,18},{20,22},{24,26},{28,30},{2,0},{... | collective-permute-start | bytes 221192 | tf_op jit(solution)/shard_map/ppermute | solution.py:741
  14.6 15.1 %all-to-all-start = ((bf16[32,24,128]{2,1,0:T(8,128)(2,1)}), bf16[32,24,128]{2,1,0:T(8,128)(2,1)S(1)}, u32[]{:S(2)}, u32[]{:S(2)}) async-start(bf16[32,24,128]{2,1,0:T(8,128)(2,1)} %get-tuple-element.69), calls=%async_computation | async-start | bytes 393216 | tf_op jit(solution)/shard_map/all_to_all | solution.py:812
